TPU v7x, 32 devices: a whole 2x2x4 slice. The times are simulated.
32 devices in a mesh: grp: 2 (over y), tgt: 8 (over z, x), src: 2 (over core).
Axes of the slice: x: 2, y: 2, z: 4, core: 2. Of those that a mesh axis runs over, the one named last changes fastest.
Arguments:
- sources: bfloat16 [131072, 32], P(('grp', 'tgt', 'src')), parts along dimension 0, may hold values from -6 to 6
- leaf_order: int32 [131072], P(('grp', 'tgt', 'src')), parts along dimension 0, may hold values from 0 to 4095, as said below
- skeleton: int32 [2048, 32], P(('grp', 'tgt')), parts along dimension 0, may hold values from 0 to 63, as said below
- interp_rows: bfloat16 [2, 2048, 32, 64], P(None, ('grp', 'tgt')), parts along dimension 1, may hold values from -0.75 to 0.75
- near_tiles: bfloat16 [2, 2048, 64, 64], P(None, ('grp', 'tgt'), 'src'), parts along dimension 1, may hold values from -0.75 to 0.75
- target_basis: bfloat16 [2, 2048, 64, 32], P(None, ('grp', 'tgt'), 'src'), parts along dimension 1, may hold values from -0.75 to 0.75
- level_maps: float32 [2, 20, 2, 32, 64], P(None, 'grp'), parts along dimension 1, may hold values from -0.5 to 0.5
Outputs:
- potential: bfloat16 [2, 131072, 32], P(None, ('grp', 'tgt', 'src')), parts along dimension 1
There are 2 independent parts, one for each index of `grp`. A program takes and returns all parts, laid end to end along the dimension named above; each array names one. Nothing has to cross between parts.
Inputs may be any that keep to these rules, and one draw needn't show every extreme that they name: `leaf_order`: each aligned block of 4096 entries is a permutation of the positions 0 .. 4095 within that block. `skeleton`: each row holds 32 distinct points of its leaf.
All inputs are finite; a program needn't handle non-finite values.
Results may differ from a plain program's by a relative error of at most 0.0045.
Values may be sent and summed in bfloat16 or wider, within the bound.
A program may use at most 64 MiB of HBM per device.

v0:
```python
import jax
import jax.numpy as jnp
from jax import lax
from jax.experimental import pallas as pl
from jax.experimental.pallas import tpu as pltpu
from jax.sharding import PartitionSpec as P

F32 = jnp.float32
BF16 = jnp.bfloat16
CHUNKS = 2
LOW = 256
VM = pl.BlockSpec(memory_space=pltpu.VMEM)
PARAMS = pltpu.CompilerParams(vmem_limit_bytes=40 * 2**20)


def from_partner(value, axis, distance):
    mask = 2**distance
    pairs = [(source, source ^ mask) for source in range(lax.axis_size(axis))]
    return lax.ppermute(value, axis, pairs)


def gather_kernel(src_ref, idx_ref, out_ref, table):
    rhs, points = src_ref.shape
    high_count = points // LOW
    boxes = out_ref.shape[2]
    per = LOW // boxes
    for high in range(high_count):
        table[pl.ds(high * rhs, rhs), :] = src_ref[:, pl.ds(high * LOW, LOW)]

    def step(g, carry):
        index = idx_ref[pl.ds(g, 1), :]
        low = index % LOW
        high_of = jnp.broadcast_to(index // LOW, (rhs, LOW))
        rows = lax.broadcasted_iota(jnp.int32, (LOW, LOW), 0)
        onehot = jnp.where(rows == low, 1.0, 0.0).astype(BF16)
        found = jnp.dot(table[...], onehot, preferred_element_type=F32)
        total = jnp.zeros((rhs, LOW), F32)
        for high in range(high_count):
            total = jnp.where(high_of == high, found[high * rhs:(high + 1) * rhs], total)
        for part in range(per):
            out_ref[g * per + part] = total[:, part * boxes:(part + 1) * boxes].astype(BF16)
        return carry

    lax.fori_loop(0, idx_ref.shape[0], step, 0)


def split(value):
    high = value.astype(BF16)
    return high, (value - high.astype(F32)).astype(BF16)


def level_block(lm_ref, level, upper):
    real = lm_ref[0, level, upper]
    imag = lm_ref[1, level, upper]
    top = jnp.concatenate([real, -imag], axis=1)
    bottom = jnp.concatenate([imag, real], axis=1)
    return jnp.concatenate([top, bottom], axis=0)


def join(lower, higher):
    half = lower.shape[0] // 2
    return jnp.concatenate([lower[:half], higher[:half], lower[half:], higher[half:]], axis=0)


def dot(a, b):
    return jnp.dot(a, b, preferred_element_type=F32)


def dot3(a, b):
    a_high, a_low = split(a)
    b_high, b_low = split(b)
    return dot(a_high, b_high) + dot(a_high, b_low) + dot(a_low, b_high)


def local_kernel(local_levels, leaves_ref, skel_ref, interp_ref, lm_ref, *rest):
    outs = rest[: 2 * CHUNKS]
    wide, weights, coeff, vals = rest[2 * CHUNKS:]
    points, rhs, boxes = leaves_ref.shape
    rank = skel_ref.shape[0]
    width = rhs // lax.axis_size("src")
    start = pl.multiple_of(lax.axis_index("src") * width, width)
    wide[...] = leaves_ref[:, pl.ds(start, width), :].astype(F32)
    block = 4
    rows = lax.broadcasted_iota(jnp.int32, (points, boxes), 0)

    def ranks(g, carry):
        for k in range(block):
            r = g * block + k
            pick = jnp.where(rows == skel_ref[pl.ds(r, 1), :], 1.0, 0.0)
            weights[2 * k] = interp_ref[0, r].astype(F32) + pick
            weights[2 * k + 1] = interp_ref[1, r].astype(F32)
        acc = [jnp.zeros((width, boxes), F32) for _ in range(2 * block)]
        for j in range(points):
            leaf = wide[j]
            for k in range(2 * block):
                acc[k] = acc[k] + weights[k, pl.ds(j, 1), :] * leaf
        for k in range(block):
            for c in range(2):
                at = pl.multiple_of((c * rank + g * block + k) * width, width)
                coeff[pl.ds(at, width), :] = acc[2 * k + c]
        return carry

    lax.fori_loop(0, rank // block, ranks, 0)
    for h in range(width):
        vals[:, h * boxes:(h + 1) * boxes] = coeff[pl.ds(h, 2 * rank, stride=width), :]
    cols = width * boxes
    lane = lax.broadcasted_iota(jnp.int32, (2 * rank, boxes), 1)
    for level in range(local_levels):
        distance = 2**level
        bit = (lane // distance) % 2 == 1
        full = jnp.concatenate([level_block(lm_ref, level, 0), level_block(lm_ref, level, 1)], axis=0)
        a_high, a_low = split(full)
        a_both = jnp.concatenate([a_high, a_high], axis=1)
        for q in range(0, cols, LOW):
            lows, highs = [], []
            for s in range(q, q + LOW, boxes):
                v = vals[:, s:s + boxes]
                lows.append(jnp.where(bit, pltpu.roll(v, distance, 1), v))
                highs.append(jnp.where(bit, v, pltpu.roll(v, boxes - distance, 1)))
            stacked = join(jnp.concatenate(lows, axis=1), jnp.concatenate(highs, axis=1))
            s_high, s_low = split(stacked)
            both = jnp.concatenate([s_high, s_low], axis=0)
            mixed = dot(a_both, both) + dot(a_low, s_high)
            for n, s in enumerate(range(q, q + LOW, boxes)):
                part = mixed[:, n * boxes:(n + 1) * boxes]
                vals[:, s:s + boxes] = jnp.where(bit, part[2 * rank:], part[:2 * rank])
    size = cols // CHUNKS
    for n in range(CHUNKS):
        piece = vals[:, n * size:(n + 1) * size]
        outs[n][...] = piece
        outs[CHUNKS + n][...] = piece.astype(BF16)


def cross_kernel(level, bit_index, lm_ref, own_ref, other_ref, *outs):
    upper = (lax.axis_index("tgt") // 2**bit_index) % 2
    block = level_block(lm_ref, level, upper)
    own = own_ref[...]
    other = other_ref[...].astype(F32)
    is_upper = jnp.broadcast_to(upper, own.shape) == 1
    stacked = join(jnp.where(is_upper, other, own), jnp.where(is_upper, own, other))
    mixed = dot3(block, stacked)
    for out in outs:
        out[...] = mixed.astype(out.dtype)


def near_kernel(leaves_ref, tiles_ref, out_ref, wide, weights):
    points, rhs, boxes = leaves_ref.shape
    wide[...] = leaves_ref[...].astype(F32)
    block = 2

    def targets(g, carry):
        for k in range(block):
            for c in range(2):
                weights[2 * k + c] = tiles_ref[c, g * block + k].astype(F32)
        acc = [jnp.zeros((rhs, boxes), F32) for _ in range(2 * block)]
        for j in range(points):
            leaf = wide[j]
            for k in range(2 * block):
                acc[k] = acc[k] + weights[k, pl.ds(j, 1), :] * leaf
        for k in range(block):
            for c in range(2):
                out_ref[c, g * block + k] = acc[2 * k + c]
        return carry

    lax.fori_loop(0, out_ref.shape[1] // block, targets, 0)


def far_kernel(basis_ref, near_ref, *rest):
    coef_refs = rest[:CHUNKS]
    out_ref, coeff, weights = rest[CHUNKS:]
    _, targets_count, rank, boxes = basis_ref.shape
    rhs = out_ref.shape[2]
    sources = coef_refs[0].shape[0]
    per = rhs // sources // CHUNKS
    for s in range(sources):
        for n in range(CHUNKS):
            for h in range(per):
                at = (s * CHUNKS + n) * per + h
                piece = coef_refs[n][s, :, h * boxes:(h + 1) * boxes].astype(F32)
                coeff[pl.ds(at, 2 * rank, stride=rhs), :] = piece
    block = 2

    def targets(g, carry):
        for k in range(block):
            for c in range(2):
                weights[2 * k + c] = basis_ref[c, g * block + k].astype(F32)
        acc = [near_ref[k % 2, g * block + k // 2] for k in range(2 * block)]
        for r in range(rank):
            real = coeff[r * rhs:(r + 1) * rhs, :]
            imag = coeff[(rank + r) * rhs:(rank + r + 1) * rhs, :]
            for k in range(block):
                w_real = weights[2 * k, pl.ds(r, 1), :]
                w_imag = weights[2 * k + 1, pl.ds(r, 1), :]
                acc[2 * k] = acc[2 * k] + w_real * real - w_imag * imag
                acc[2 * k + 1] = acc[2 * k + 1] + w_real * imag + w_imag * real
        for k in range(block):
            for c in range(2):
                out_ref[c, g * block + k] = acc[2 * k + c].astype(BF16)
        return carry

    lax.fori_loop(0, targets_count // block, targets, 0)


def call(body, out_shape, scratch, operands, flops=0, moved=0):
    many = isinstance(out_shape, (list, tuple))
    return pl.pallas_call(
        body,
        out_shape=out_shape,
        in_specs=[VM] * len(operands),
        out_specs=[VM] * len(out_shape) if many else VM,
        scratch_shapes=scratch,
        compiler_params=PARAMS,
        cost_estimate=pl.CostEstimate(flops=flops, bytes_accessed=moved, transcendentals=0),
    )(*operands)


def on_device(sources, leaf_order, skeleton, interp_rows, near_tiles, target_basis, level_maps):
    tgt_count = lax.axis_size("tgt")
    src_count = lax.axis_size("src")
    point_count, rhs = sources.shape
    boxes, rank = skeleton.shape
    leaf = interp_rows.shape[3]
    half = leaf // src_count
    width = rhs // src_count
    cols = width * boxes
    size = cols // CHUNKS
    shape = jax.ShapeDtypeStruct
    vmem = pltpu.VMEM

    index = leaf_order.reshape(boxes, half).T.reshape(point_count // LOW, LOW)
    halves = call(
        gather_kernel, shape((half, rhs, boxes), BF16),
        [vmem((point_count // LOW * rhs, LOW), BF16)], (sources.T, index),
        2 * point_count * rhs * point_count, 2**20,
    )
    leaves = lax.all_gather(halves, "src", axis=0, tiled=True)
    local_levels = boxes.bit_length() - 1
    cross_count = tgt_count.bit_length() - 1
    made = call(
        lambda *refs: local_kernel(local_levels, *refs),
        [shape((2 * rank, size), F32)] * CHUNKS + [shape((2 * rank, size), BF16)] * CHUNKS,
        [
            vmem((leaf, width, boxes), F32), vmem((8, leaf, boxes), F32),
            vmem((2 * rank * width, boxes), F32), vmem((2 * rank, cols), F32),
        ],
        (leaves, skeleton.T, interp_rows.transpose(0, 2, 3, 1), level_maps),
        10**9, 2**22,
    )
    values, narrow = list(made[:CHUNKS]), list(made[CHUNKS:])
    near = call(
        near_kernel, shape((2, half, rhs, boxes), F32),
        [vmem((leaf, rhs, boxes), F32), vmem((4, leaf, boxes), F32)],
        (leaves, near_tiles.transpose(0, 2, 3, 1)),
        5 * 10**9, 2**24,
    )
    for bit_index in range(cross_count):
        last = bit_index == cross_count - 1
        level = local_levels + bit_index
        others = [from_partner(piece, "tgt", bit_index) for piece in narrow]
        for n in range(CHUNKS):
            out = [shape((2 * rank, size), BF16)]
            if not last:
                out.append(shape((2 * rank, size), F32))
            mixed = call(
                lambda *refs: cross_kernel(level, bit_index, *refs), out, [],
                (level_maps, values[n], others[n]), 10**8, 2**20,
            )
            narrow[n] = mixed[0]
            if not last:
                values[n] = mixed[1]
    rounded = [lax.all_gather(piece, "src", axis=0) for piece in narrow]
    field = call(
        far_kernel, shape((2, half, rhs, boxes), BF16),
        [vmem((2 * rank * rhs, boxes), F32), vmem((4, rank, boxes), F32)],
        (target_basis.transpose(0, 2, 3, 1), near, *rounded),
        5 * 10**9, 2**22,
    )
    return field.transpose(0, 3, 1, 2).reshape(2, boxes * half, rhs)


def solution(mesh):
    return jax.shard_map(
        on_device,
        mesh=mesh,
        in_specs=(
            P(("grp", "tgt", "src"), None),
            P(("grp", "tgt", "src")),
            P(("grp", "tgt"), None),
            P(None, ("grp", "tgt"), None, None),
            P(None, ("grp", "tgt"), "src", None),
            P(None, ("grp", "tgt"), "src", None),
            P(None, "grp", None, None, None),
        ),
        out_specs=P(None, ("grp", "tgt", "src"), None),
        check_vma=False,
    )
```

profile of v0, /device:TPU:0, one launch (start us, length us, event | category | flops | bytes accessed | tf_op | source)
XLA Modules:
  0.0 53.7 jit_solution(3209298728421369597)
XLA Ops:
  0.0 0.8 %reshape.9 = s32[128,32]{1,0:T(8,128)S(1)} reshape(s32[4096]{0:T(1024)} %param.8) | data formatting | bytes 32768 | tf_op jit(solution)/shard_map/reshape | solution.py:230
  0.8 0.1 copy.10
  0.9 0.0 copy-start.4
  0.9 0.9 %copy-done.4 = bf16[4096,32]{0,1:T(8,128)(2,1)S(1)} copy-done((bf16[4096,32]{0,1:T(8,128)(2,1)S(1)}, bf16[4096,32]{0,1:T(8,128)(2,1)}, u32[]{:S(2)}) %copy-start.4) | copy-done | bytes 262168
  1.8 0.0 copy-start
  1.8 0.0 copy-start.1
  1.8 0.0 copy-start.5
  1.8 4.0 %shard_map.73 = bf16[32,32,128]{2,1,0:T(8,128)(2,1)S(1)} custom-call(bf16[32,4096]{1,0:T(8,128)(2,1)S(1)} %bitcast.19, s32[16,256]{1,0:T(8,128)S(1)} %reshape.10.idx_ref), custom_call_target="tpu_custom_call" | custom-call | flops 1073741824 | bytes 1048576 | tf_op jit(solution)/shard_map/pallas_call | solution.py:206
  5.8 2.3 %all_gather.15.leaves_ref.refs_0_ = bf16[64,32,128]{2,1,0:T(8,128)(2,1)S(1)} all-gather(bf16[32,32,128]{2,1,0:T(8,128)(2,1)S(1)} %shard_map.73), channel_id=1, replica_groups=mesh['grp'=2,'tgt'=8,'src'=2] {'src'}, dimensions={0}, use_global_device_ids=true | all-gather | bytes 786432 | tf_op jit(solution)/shard_map/all_gather | solution.py:236
  8.1 0.0 copy-done
  8.1 0.0 copy-done.1
  8.1 0.0 copy-done.5
  8.1 5.0 %shard_map.75 = (f32[64,1024]{1,0:T(8,128)S(1)}, f32[64,1024]{1,0:T(8,128)S(1)}, bf16[64,1024]{1,0:T(8,128)(2,1)S(1)}, bf16[64,1024]{1,0:T(8,128)(2,1)S(1)}) custom-call(bf16[64,32,128]{2,1,0:T(8,128)(2,1)S(1)} %all_gather.15.leaves_ref.refs_0_, s32[32,128]{1,0:T(8,128)S(1)} %bitcast.20, bf16[2,32,64,128]{3,2,1,0:T(8,128)(2,1)S(1)} %bitcast.16, ...), custom_call_target="tpu_custom_call" | custom-call | flops 1000000000 | bytes 4194304 | tf_op jit(solution)/shard_map/pallas_call | solution.py:206
  13.1 2.9 %collective-permute-start = (bf16[64,1024]{1,0:T(8,128)(2,1)S(1)}, bf16[64,1024]{1,0:T(8,128)(2,1)S(1)}, u32[]{:S(2)}, u32[]{:S(2)}) collective-permute-start(bf16[64,1024]{1,0:T(8,128)(2,1)S(1)} %get-tuple-element.18), channel_id=1, source_target_pairs={{0,2},{2,0},{4,6},{6,4},{8,10},{10,8},{12,14},{14,12},{1,3},{3,1},... | collective-permute-start | bytes 393224 | tf_op jit(solution)/shard_map/ppermute | solution.py:19
  16.1 0.1 collective-permute-start.3
  16.1 4.2 %collective-permute-done.refs_2_ = bf16[64,1024]{1,0:T(8,128)(2,1)S(1)} collective-permute-done((bf16[64,1024]{1,0:T(8,128)(2,1)S(1)}, bf16[64,1024]{1,0:T(8,128)(2,1)S(1)}, u32[]{:S(2)}, u32[]{:S(2)}) %collective-permute-start) | collective-permute-done | bytes 131104 | tf_op jit(solution)/shard_map/ppermute | solution.py:19
  20.4 0.0 copy-start.2
  20.4 0.3 shard_map.76
  20.7 2.2 %collective-permute-start.1 = (bf16[64,1024]{1,0:T(8,128)(2,1)S(1)}, bf16[64,1024]{1,0:T(8,128)(2,1)S(1)}, u32[]{:S(2)}, u32[]{:S(2)}) collective-permute-start(bf16[64,1024]{1,0:T(8,128)(2,1)S(1)} %get-tuple-element.20), channel_id=1, source_target_pairs={{0,4},{2,6},{4,0},{6,2},{8,12},{10,14},{12,8},{14,10},{1,5},{3,7},... | collective-permute-start | bytes 393224 | tf_op jit(solution)/shard_map/ppermute | solution.py:19
  22.9 0.0 collective-permute-done.3.refs_2_
  22.9 0.3 shard_map.79
  23.3 1.6 %collective-permute-start.4 = (bf16[64,1024]{1,0:T(8,128)(2,1)S(1)}, bf16[64,1024]{1,0:T(8,128)(2,1)S(1)}, u32[]{:S(2)}, u32[]{:S(2)}) collective-permute-start(bf16[64,1024]{1,0:T(8,128)(2,1)S(1)} %get-tuple-element.26), channel_id=1, source_target_pairs={{0,4},{2,6},{4,0},{6,2},{8,12},{10,14},{12,8},{14,10},{1,5},{3,7},... | collective-permute-start | bytes 393224 | tf_op jit(solution)/shard_map/ppermute | solution.py:19
  24.9 1.6 %collective-permute-done.1.refs_2_ = bf16[64,1024]{1,0:T(8,128)(2,1)S(1)} collective-permute-done((bf16[64,1024]{1,0:T(8,128)(2,1)S(1)}, bf16[64,1024]{1,0:T(8,128)(2,1)S(1)}, u32[]{:S(2)}, u32[]{:S(2)}) %collective-permute-start.1) | collective-permute-done | bytes 131104 | tf_op jit(solution)/shard_map/ppermute | solution.py:19
  26.5 0.3 shard_map.77
  26.8 3.6 %collective-permute-start.2 = (bf16[64,1024]{1,0:T(8,128)(2,1)S(1)}, bf16[64,1024]{1,0:T(8,128)(2,1)S(1)}, u32[]{:S(2)}, u32[]{:S(2)}) collective-permute-start(bf16[64,1024]{1,0:T(8,128)(2,1)S(1)} %get-tuple-element.22), channel_id=1, source_target_pairs={{0,8},{2,10},{4,12},{6,14},{8,0},{10,2},{12,4},{14,6},{1,9},{3,11}... | collective-permute-start | bytes 393224 | tf_op jit(solution)/shard_map/ppermute | solution.py:19
  30.4 0.0 collective-permute-done.4.refs_2_
  30.4 0.3 shard_map.80
  30.7 2.5 %collective-permute-start.5 = (bf16[64,1024]{1,0:T(8,128)(2,1)S(1)}, bf16[64,1024]{1,0:T(8,128)(2,1)S(1)}, u32[]{:S(2)}, u32[]{:S(2)}) collective-permute-start(bf16[64,1024]{1,0:T(8,128)(2,1)S(1)} %get-tuple-element.28), channel_id=1, source_target_pairs={{0,8},{2,10},{4,12},{6,14},{8,0},{10,2},{12,4},{14,6},{1,9},{3,11}... | collective-permute-start | bytes 393224 | tf_op jit(solution)/shard_map/ppermute | solution.py:19
  33.2 0.0 copy-done.2
  33.2 4.6 %shard_map.74.near_ref = f32[2,32,32,128]{3,2,1,0:T(8,128)S(1)} custom-call(bf16[64,32,128]{2,1,0:T(8,128)(2,1)S(1)} %all_gather.15.leaves_ref.refs_0_, bf16[2,32,64,128]{3,2,1,0:T(8,128)(2,1)S(1)} %bitcast.17), custom_call_target="tpu_custom_call" | custom-call | flops 5000000000 | bytes 16777216 | tf_op jit(solution)/shard_map/pallas_call | solution.py:206
  37.8 0.0 copy-start.3
  37.8 1.6 %collective-permute-done.2.refs_2_ = bf16[64,1024]{1,0:T(8,128)(2,1)S(1)} collective-permute-done((bf16[64,1024]{1,0:T(8,128)(2,1)S(1)}, bf16[64,1024]{1,0:T(8,128)(2,1)S(1)}, u32[]{:S(2)}, u32[]{:S(2)}) %collective-permute-start.2) | collective-permute-done | bytes 131104 | tf_op jit(solution)/shard_map/ppermute | solution.py:19
  39.4 0.3 shard_map.78
  39.7 2.0 %all-gather = bf16[128,1024]{1,0:T(8,128)(2,1)S(1)} all-gather(bf16[64,1024]{1,0:T(8,128)(2,1)S(1)} %shard_map.78), channel_id=2, replica_groups=mesh['grp'=2,'tgt'=8,'src'=2] {'src'}, dimensions={0}, use_global_device_ids=true | all-gather | bytes 393216 | tf_op jit(solution)/shard_map/all_gather | solution.py:271
  41.7 0.0 collective-permute-done.5.refs_2_
  41.7 0.3 shard_map.81
  42.1 2.0 %all-gather.1 = bf16[128,1024]{1,0:T(8,128)(2,1)S(1)} all-gather(bf16[64,1024]{1,0:T(8,128)(2,1)S(1)} %shard_map.81), channel_id=3, replica_groups=mesh['grp'=2,'tgt'=8,'src'=2] {'src'}, dimensions={0}, use_global_device_ids=true | all-gather | bytes 393216 | tf_op jit(solution)/shard_map/all_gather | solution.py:271
  44.1 0.0 copy-done.3
  44.1 5.5 %shard_map.82 = bf16[2,32,32,128]{3,2,1,0:T(8,128)(2,1)S(1)} custom-call(bf16[2,32,32,128]{3,2,1,0:T(8,128)(2,1)S(1)} %bitcast.18, f32[2,32,32,128]{3,2,1,0:T(8,128)S(1)} %shard_map.74.near_ref, bf16[2,64,1024]{2,1,0:T(8,128)(2,1)S(1)} %bitcast.14, bf16[2,64,1024]{2,1,0:T(8,128)(2,1)S(1)} %bitcast.15), custom_call_target="tpu_custom_call" | custom-call | flops 5000000000 | bytes 4194304 | tf_op jit(solution)/shard_map/pallas_call | solution.py:206
  49.6 1.1 %copy.11 = bf16[2,128,32,32]{2,1,3,0:T(8,128)(2,1)S(1)} copy(bf16[2,128,32,32]{1,3,2,0:T(8,128)(2,1)S(1)} %bitcast.13) | data formatting | bytes 1048576 | tf_op jit(solution)/shard_map/transpose | solution.py:278
  50.7 3.0 %reshape.11 = bf16[2,4096,32]{1,2,0:T(8,128)(2,1)} reshape(bf16[2,128,32,32]{2,1,3,0:T(8,128)(2,1)S(1)} %copy.11) | data formatting | bytes 1048576 | tf_op jit(solution)/shard_map/reshape | solution.py:278
  (1 shorter events, 0.0 us)
Async XLA Ops:
  0.9 1.0 %copy-start.4 = (bf16[4096,32]{0,1:T(8,128)(2,1)S(1)}, bf16[4096,32]{0,1:T(8,128)(2,1)}, u32[]{:S(2)}) copy-start(bf16[4096,32]{0,1:T(8,128)(2,1)} %param.7) | copy-start | bytes 786436
  1.8 6.2 %copy-start = (f32[2,10,2,32,64]{4,3,2,1,0:T(8,128)S(1)}, f32[2,10,2,32,64]{4,3,2,1,0:T(8,128)}, u32[]{:S(2)}) copy-start(f32[2,10,2,32,64]{4,3,2,1,0:T(8,128)} %refs_0_.11) | copy-start | bytes 983044
  1.8 6.3 %copy-start.1 = (bf16[2,128,32,64]{1,3,2,0:T(8,128)(2,1)S(1)}, bf16[2,128,32,64]{1,3,2,0:T(8,128)(2,1)}, u32[]{:S(2)}) copy-start(bf16[2,128,32,64]{1,3,2,0:T(8,128)(2,1)} %param.10) | copy-start | bytes 3145732
  1.8 6.3 %copy-start.5 = (s32[128,32]{0,1:T(8,128)S(1)}, s32[128,32]{0,1:T(8,128)}, u32[]{:S(2)}) copy-start(s32[128,32]{0,1:T(8,128)} %param.9) | copy-start | bytes 49156
  13.1 7.2 %collective-permute-start = (bf16[64,1024]{1,0:T(8,128)(2,1)S(1)}, bf16[64,1024]{1,0:T(8,128)(2,1)S(1)}, u32[]{:S(2)}, u32[]{:S(2)}) collective-permute-start(bf16[64,1024]{1,0:T(8,128)(2,1)S(1)} %get-tuple-element.18), channel_id=1, source_target_pairs={{0,2},{2,0},{4,6},{6,4},{8,10},{10,8},{12,14},{14,12},{1,3},{3,1},... | collective-permute-start | bytes 393224 | tf_op jit(solution)/shard_map/ppermute | solution.py:19
  16.1 6.9 %collective-permute-start.3 = (bf16[64,1024]{1,0:T(8,128)(2,1)S(1)}, bf16[64,1024]{1,0:T(8,128)(2,1)S(1)}, u32[]{:S(2)}, u32[]{:S(2)}) collective-permute-start(bf16[64,1024]{1,0:T(8,128)(2,1)S(1)} %get-tuple-element.24), channel_id=1, source_target_pairs={{0,2},{2,0},{4,6},{6,4},{8,10},{10,8},{12,14},{14,12},{1,3},{3,1},... | collective-permute-start | bytes 393224 | tf_op jit(solution)/shard_map/ppermute | solution.py:19
  20.4 12.8 %copy-start.2 = (bf16[2,128,32,64]{1,3,2,0:T(8,128)(2,1)S(1)}, bf16[2,128,32,64]{1,3,2,0:T(8,128)(2,1)}, u32[]{:S(2)}) copy-start(bf16[2,128,32,64]{1,3,2,0:T(8,128)(2,1)} %param.11) | copy-start | bytes 3145732
  20.7 5.8 %collective-permute-start.1 = (bf16[64,1024]{1,0:T(8,128)(2,1)S(1)}, bf16[64,1024]{1,0:T(8,128)(2,1)S(1)}, u32[]{:S(2)}, u32[]{:S(2)}) collective-permute-start(bf16[64,1024]{1,0:T(8,128)(2,1)S(1)} %get-tuple-element.20), channel_id=1, source_target_pairs={{0,4},{2,6},{4,0},{6,2},{8,12},{10,14},{12,8},{14,10},{1,5},{3,7},... | collective-permute-start | bytes 393224 | tf_op jit(solution)/shard_map/ppermute | solution.py:19
  23.3 7.1 %collective-permute-start.4 = (bf16[64,1024]{1,0:T(8,128)(2,1)S(1)}, bf16[64,1024]{1,0:T(8,128)(2,1)S(1)}, u32[]{:S(2)}, u32[]{:S(2)}) collective-permute-start(bf16[64,1024]{1,0:T(8,128)(2,1)S(1)} %get-tuple-element.26), channel_id=1, source_target_pairs={{0,4},{2,6},{4,0},{6,2},{8,12},{10,14},{12,8},{14,10},{1,5},{3,7},... | collective-permute-start | bytes 393224 | tf_op jit(solution)/shard_map/ppermute | solution.py:19
  26.8 12.6 %collective-permute-start.2 = (bf16[64,1024]{1,0:T(8,128)(2,1)S(1)}, bf16[64,1024]{1,0:T(8,128)(2,1)S(1)}, u32[]{:S(2)}, u32[]{:S(2)}) collective-permute-start(bf16[64,1024]{1,0:T(8,128)(2,1)S(1)} %get-tuple-element.22), channel_id=1, source_target_pairs={{0,8},{2,10},{4,12},{6,14},{8,0},{10,2},{12,4},{14,6},{1,9},{3,11}... | collective-permute-start | bytes 393224 | tf_op jit(solution)/shard_map/ppermute | solution.py:19
  30.7 11.0 %collective-permute-start.5 = (bf16[64,1024]{1,0:T(8,128)(2,1)S(1)}, bf16[64,1024]{1,0:T(8,128)(2,1)S(1)}, u32[]{:S(2)}, u32[]{:S(2)}) collective-permute-start(bf16[64,1024]{1,0:T(8,128)(2,1)S(1)} %get-tuple-element.28), channel_id=1, source_target_pairs={{0,8},{2,10},{4,12},{6,14},{8,0},{10,2},{12,4},{14,6},{1,9},{3,11}... | collective-permute-start | bytes 393224 | tf_op jit(solution)/shard_map/ppermute | solution.py:19
  37.8 6.3 %copy-start.3 = (bf16[2,128,32,32]{1,3,2,0:T(8,128)(2,1)S(1)}, bf16[2,128,32,32]{1,3,2,0:T(8,128)(2,1)}, u32[]{:S(2)}) copy-start(bf16[2,128,32,32]{1,3,2,0:T(8,128)(2,1)} %param.12) | copy-start | bytes 1572868
where the time goes:
time: 54 us; the launch traced here: 53.7 us
  Pallas kernels  21.1 us (39%)
  starting transfers between devices  12.9 us (24%)
  waiting for transfers between devices  7.4 us (14%)
  blocking collectives  6.25 us (12%)
  local copies, waits for them, and re-layouts  5.94 us (11%)
    pallas_call x10, Pallas kernels, call(): pl.pallas_call(body, out_shape=out_shape, in_specs=[VM] * len(operands),...  21.1 us
    ppermute x6, starting transfers between devices, from_partner(): return lax.ppermute(value, axis, pairs)  12.9 us
    ppermute x6, waiting for transfers between devices, from_partner(): return lax.ppermute(value, axis, pairs)  7.4 us
    all_gather x2, blocking collectives, on_device(): rounded = [lax.all_gather(piece, 'src', axis=0) for piece in narrow]  3.99 us
    reshape x1, local copies, waits for them, and re-layouts, on_device(): return field.transpose(0, 3, 1, 2).reshape(2, boxes * half, rhs)  2.97 us
    all_gather x1, blocking collectives, on_device(): leaves = lax.all_gather(halves, 'src', axis=0, tiled=True)  2.26 us
    transpose x1, local copies, waits for them, and re-layouts, on_device(): return field.transpose(0, 3, 1, 2).reshape(2, boxes * half, rhs)  1.13 us
  transfers between devices with their start and end apart: 6, of which 3 were waited for; matrix products, arithmetic and copies ran while one was open for 0% of the time, Pallas kernels for 12%

commit v1 on v0

v1 whole, which is shorter than its diff:
```python
import jax
import jax.numpy as jnp
from jax import lax
from jax.experimental import pallas as pl
from jax.experimental.pallas import tpu as pltpu
from jax.sharding import PartitionSpec as P

F32 = jnp.float32
BF16 = jnp.bfloat16
CHUNKS = 4
LOW = 256
VM = pl.BlockSpec(memory_space=pltpu.VMEM)
PARAMS = pltpu.CompilerParams(vmem_limit_bytes=40 * 2**20)


def gather_kernel(src_ref, idx_ref, out_ref, table):
    rhs, points = src_ref.shape
    high_count = points // LOW
    boxes = out_ref.shape[2]
    per = LOW // boxes
    for high in range(high_count):
        table[pl.ds(high * rhs, rhs), :] = src_ref[:, pl.ds(high * LOW, LOW)]

    def step(g, carry):
        index = idx_ref[pl.ds(g, 1), :]
        low = index % LOW
        high_of = jnp.broadcast_to(index // LOW, (rhs, LOW))
        rows = lax.broadcasted_iota(jnp.int32, (LOW, LOW), 0)
        onehot = jnp.where(rows == low, 1.0, 0.0).astype(BF16)
        found = jnp.dot(table[...], onehot, preferred_element_type=F32)
        total = jnp.zeros((rhs, LOW), F32)
        for high in range(high_count):
            total = jnp.where(high_of == high, found[high * rhs:(high + 1) * rhs], total)
        for part in range(per):
            out_ref[g * per + part] = total[:, part * boxes:(part + 1) * boxes].astype(BF16)
        return carry

    lax.fori_loop(0, idx_ref.shape[0], step, 0)


def split(value):
    high = value.astype(BF16)
    return high, (value - high.astype(F32)).astype(BF16)


def level_block(lm_ref, level, upper):
    real = lm_ref[0, level, upper]
    imag = lm_ref[1, level, upper]
    top = jnp.concatenate([real, -imag], axis=1)
    bottom = jnp.concatenate([imag, real], axis=1)
    return jnp.concatenate([top, bottom], axis=0)


def join(lower, higher):
    half = lower.shape[0] // 2
    return jnp.concatenate([lower[:half], higher[:half], lower[half:], higher[half:]], axis=0)


def dot(a, b):
    return jnp.dot(a, b, preferred_element_type=F32)


def dot3(a, b):
    a_high, a_low = split(a)
    b_high, b_low = split(b)
    return dot(a_high, b_high) + dot(a_high, b_low) + dot(a_low, b_high)


def local_kernel(local_levels, leaves_ref, skel_ref, interp_ref, lm_ref, vals,
                 wide, weights, coeff):
    points, rhs, boxes = leaves_ref.shape
    rank = skel_ref.shape[0]
    width = rhs // lax.axis_size("src")
    start = pl.multiple_of(lax.axis_index("src") * width, width)
    wide[...] = leaves_ref[:, pl.ds(start, width), :].astype(F32)
    block = 4
    rows = lax.broadcasted_iota(jnp.int32, (points, boxes), 0)

    def ranks(g, carry):
        for k in range(block):
            r = g * block + k
            pick = jnp.where(rows == skel_ref[pl.ds(r, 1), :], 1.0, 0.0)
            weights[2 * k] = interp_ref[0, r].astype(F32) + pick
            weights[2 * k + 1] = interp_ref[1, r].astype(F32)
        acc = [jnp.zeros((width, boxes), F32) for _ in range(2 * block)]
        for j in range(points):
            leaf = wide[j]
            for k in range(2 * block):
                acc[k] = acc[k] + weights[k, pl.ds(j, 1), :] * leaf
        for k in range(block):
            for c in range(2):
                at = pl.multiple_of((c * rank + g * block + k) * width, width)
                coeff[pl.ds(at, width), :] = acc[2 * k + c]
        return carry

    lax.fori_loop(0, rank // block, ranks, 0)
    for h in range(width):
        vals[:, h * boxes:(h + 1) * boxes] = coeff[pl.ds(h, 2 * rank, stride=width), :]
    cols = width * boxes
    lane = lax.broadcasted_iota(jnp.int32, (2 * rank, boxes), 1)
    for level in range(local_levels):
        distance = 2**level
        bit = (lane // distance) % 2 == 1
        full = jnp.concatenate([level_block(lm_ref, level, 0), level_block(lm_ref, level, 1)], axis=0)
        a_high, a_low = split(full)
        a_both = jnp.concatenate([a_high, a_high], axis=1)
        for q in range(0, cols, LOW):
            lows, highs = [], []
            for s in range(q, q + LOW, boxes):
                v = vals[:, s:s + boxes]
                lows.append(jnp.where(bit, pltpu.roll(v, distance, 1), v))
                highs.append(jnp.where(bit, v, pltpu.roll(v, boxes - distance, 1)))
            stacked = join(jnp.concatenate(lows, axis=1), jnp.concatenate(highs, axis=1))
            s_high, s_low = split(stacked)
            both = jnp.concatenate([s_high, s_low], axis=0)
            mixed = dot(a_both, both) + dot(a_low, s_high)
            for n, s in enumerate(range(q, q + LOW, boxes)):
                part = mixed[:, n * boxes:(n + 1) * boxes]
                vals[:, s:s + boxes] = jnp.where(bit, part[2 * rank:], part[:2 * rank])


def partner_of(axis, bit_index):
    me = lax.axis_index(axis)
    mask = 2**bit_index
    return {axis: me + mask - 2 * mask * ((me // mask) % 2)}


def plan(bit_count):
    steps = [(bit, n) for bit in range(bit_count) for n in range(CHUNKS)]
    return sorted(steps, key=lambda at: at[1] + 1.5 * at[0] + (at[0] == bit_count - 1))


def cross_kernel(local_levels, bit_count, lm_ref, vals_ref, leaves_ref, tiles_ref, basis_ref, out_ref,
                 vals, sent, came, mine, theirs, wide, weights, near, basis, coeff, send_sem, recv_sem):
    points, rhs, boxes = leaves_ref.shape
    _, target_count, rank, _ = basis_ref.shape
    size = sent.shape[3]
    per = size // boxes
    group = coeff.shape[1] // (2 * rank)
    sources = group // per
    src_first = jnp.broadcast_to(lax.axis_index("src"), (2 * rank, size)) == 0

    barrier = pltpu.get_barrier_semaphore()
    peers = [partner_of("tgt", bit) for bit in range(bit_count)] + [partner_of("src", 0)]
    for peer in peers:
        pl.semaphore_signal(barrier, inc=1, device_id=peer, device_id_type=pl.DeviceIdType.MESH)
    pl.semaphore_wait(barrier, len(peers))

    def copy_of(bit, n):
        inside = bit < bit_count
        return pltpu.make_async_remote_copy(
            src_ref=sent.at[bit, n] if inside else mine.at[n],
            dst_ref=came.at[bit, n] if inside else theirs.at[n],
            send_sem=send_sem.at[bit, n],
            recv_sem=recv_sem.at[bit, n],
            device_id=peers[bit],
            device_id_type=pl.DeviceIdType.MESH,
        )

    for n in range(CHUNKS):
        piece = vals_ref[:, n * size:(n + 1) * size]
        sent[0, n] = piece.astype(BF16)
        copy_of(0, n).start()
        vals[n] = piece

    for n in range(CHUNKS):
        for s in range(sources):
            start = s * per * CHUNKS + n * per
            wide[:, n * group + s * per:n * group + (s + 1) * per, :] = (
                leaves_ref[...].astype(F32)[:, start:start + per, :]
            )

    block = weights.shape[0] // 2

    def near_step(g, carry):
        for k in range(block):
            for c in range(2):
                weights[2 * k + c] = tiles_ref[c, g * block + k].astype(F32)
        acc = jnp.zeros((2 * block, rhs, boxes), F32)
        for j in range(points):
            acc = acc + weights[:, j:j + 1, :] * wide[j][None]
        for k in range(block):
            for c in range(2):
                for n in range(CHUNKS):
                    near[n, c, g * block + k] = acc[2 * k + c, n * group:(n + 1) * group]
        return carry

    near_total = target_count // block
    done = 0

    def near_part(count):
        nonlocal done
        end = min(near_total, done + count)
        if end > done:
            lax.fori_loop(done, end, near_step, 0)
        done = end

    def far_part(n):
        copy_of(bit_count, n).wait_recv()
        own = mine[n].astype(F32)
        other = theirs[n].astype(F32)
        for s, piece in enumerate((jnp.where(src_first, own, other), jnp.where(src_first, other, own))):
            for h in range(per):
                coeff[n, pl.ds(s * per + h, 2 * rank, stride=group), :] = piece[:, h * boxes:(h + 1) * boxes]
        many = 8

        def far_step(g, carry):
            rows = pl.ds(pl.multiple_of(g * many, many), many)
            real_acc = near[n, 0, rows]
            imag_acc = near[n, 1, rows]
            for r in range(rank):
                real = coeff[n, r * group:(r + 1) * group, :][None]
                imag = coeff[n, (rank + r) * group:(rank + r + 1) * group, :][None]
                w_real = basis[0, rows, r:r + 1, :]
                w_imag = basis[1, rows, r:r + 1, :]
                real_acc = real_acc + w_real * real - w_imag * imag
                imag_acc = imag_acc + w_real * imag + w_imag * real
            out_ref[n, 0, rows] = real_acc.astype(BF16)
            out_ref[n, 1, rows] = imag_acc.astype(BF16)
            return carry

        lax.fori_loop(0, target_count // many, far_step, 0)

    slots = [6, 3, 3, 2, 2]
    for at, (bit, n) in enumerate(plan(bit_count)):
        last = bit == bit_count - 1
        if last and n == 0:
            near_part(near_total)
            basis[...] = basis_ref[...].astype(F32)
        elif at < len(slots):
            near_part(slots[at])
        copy_of(bit, n).wait_recv()
        upper = (lax.axis_index("tgt") // 2**bit) % 2
        own = vals[n]
        other = came[bit, n].astype(F32)
        is_upper = jnp.broadcast_to(upper, own.shape) == 1
        stacked = join(jnp.where(is_upper, other, own), jnp.where(is_upper, own, other))
        mixed = dot3(level_block(lm_ref, local_levels + bit, upper), stacked)
        if last:
            mine[n] = mixed.astype(BF16)
        else:
            vals[n] = mixed
            sent[bit + 1, n] = mixed.astype(BF16)
        copy_of(bit + 1, n).start()
        if last:
            far_part(n)
    for bit in range(bit_count + 1):
        for n in range(CHUNKS):
            copy_of(bit, n).wait_send()


def call(body, out_shape, scratch, operands, params=PARAMS):
    return pl.pallas_call(
        body,
        out_shape=out_shape,
        in_specs=[VM] * len(operands),
        out_specs=VM,
        scratch_shapes=scratch,
        compiler_params=params,
    )(*operands)


def on_device(sources, leaf_order, skeleton, interp_rows, near_tiles, target_basis, level_maps):
    tgt_count = lax.axis_size("tgt")
    src_count = lax.axis_size("src")
    point_count, rhs = sources.shape
    boxes, rank = skeleton.shape
    leaf = interp_rows.shape[3]
    half = leaf // src_count
    width = rhs // src_count
    cols = width * boxes
    size = cols // CHUNKS
    shape = jax.ShapeDtypeStruct
    vmem = pltpu.VMEM

    index = leaf_order.reshape(boxes, half).T.reshape(point_count // LOW, LOW)
    halves = call(
        gather_kernel, shape((half, rhs, boxes), BF16),
        [vmem((point_count // LOW * rhs, LOW), BF16)], (sources.T, index),
    )
    leaves = lax.all_gather(halves, "src", axis=0, tiled=True)
    local_levels = boxes.bit_length() - 1
    cross_count = tgt_count.bit_length() - 1
    values = call(
        lambda *refs: local_kernel(local_levels, *refs),
        shape((2 * rank, cols), F32),
        [
            vmem((leaf, width, boxes), F32), vmem((8, leaf, boxes), F32),
            vmem((2 * rank * width, boxes), F32),
        ],
        (leaves, skeleton.T, interp_rows.transpose(0, 2, 3, 1), level_maps),
    )
    group = rhs // CHUNKS
    field = call(
        lambda *refs: cross_kernel(local_levels, cross_count, *refs),
        shape((CHUNKS, 2, half, group, boxes), BF16),
        [
            vmem((CHUNKS, 2 * rank, size), F32),
            vmem((cross_count, CHUNKS, 2 * rank, size), BF16),
            vmem((cross_count, CHUNKS, 2 * rank, size), BF16),
            vmem((CHUNKS, 2 * rank, size), BF16),
            vmem((CHUNKS, 2 * rank, size), BF16),
            vmem((leaf, rhs, boxes), F32),
            vmem((4, leaf, boxes), F32),
            vmem((CHUNKS, 2, half, group, boxes), F32),
            vmem((2, half, rank, boxes), F32),
            vmem((CHUNKS, 2 * rank * group, boxes), F32),
            pltpu.SemaphoreType.DMA((cross_count + 1, CHUNKS)),
            pltpu.SemaphoreType.DMA((cross_count + 1, CHUNKS)),
        ],
        (level_maps, values, leaves, near_tiles.transpose(0, 2, 3, 1), target_basis.transpose(0, 2, 3, 1)),
        pltpu.CompilerParams(vmem_limit_bytes=40 * 2**20, collective_id=0, has_side_effects=True),
    )
    field = field.reshape(CHUNKS, 2, half, src_count, group // src_count, boxes)
    return field.transpose(1, 5, 2, 3, 0, 4).reshape(2, boxes * half, rhs)


def solution(mesh):
    return jax.shard_map(
        on_device,
        mesh=mesh,
        in_specs=(
            P(("grp", "tgt", "src"), None),
            P(("grp", "tgt", "src")),
            P(("grp", "tgt"), None),
            P(None, ("grp", "tgt"), None, None),
            P(None, ("grp", "tgt"), "src", None),
            P(None, ("grp", "tgt"), "src", None),
            P(None, "grp", None, None, None),
        ),
        out_specs=P(None, ("grp", "tgt", "src"), None),
        check_vma=False,
    )
```

time: 54 us -> 50.7 us (0.939)
  Pallas kernels: 21.1 us -> 39 us
  starting transfers between devices: 12.9 us -> 0 us
  waiting for transfers between devices: 7.4 us -> 0 us
  blocking collectives: 6.25 us -> 2.26 us
  local copies, waits for them, and re-layouts: 5.94 us -> 8.98 us
    pallas_call x10 -> x3, Pallas kernels: 21.1 us -> 39 us  [call(): pl.pallas_call(body, out_shape=out_shape, in_specs=[VM] * len(operands),...]
    ppermute x6 -> x0, starting transfers between devices: 12.9 us -> none  [from_partner(): return lax.ppermute(value, axis, pairs)]
    ppermute x6 -> x0, waiting for transfers between devices: 7.4 us -> none  [from_partner(): return lax.ppermute(value, axis, pairs)]
    all_gather x2 -> x0, blocking collectives: 3.99 us -> none  [on_device(): rounded = [lax.all_gather(piece, 'src', axis=0) for piece in narrow]]
    unnamed x12 -> x14, local copies, waits for them, and re-layouts: 0.97 us -> 4.06 us
    transpose x1 -> x0, local copies, waits for them, and re-layouts: 1.13 us -> none  [on_device(): return field.transpose(0, 3, 1, 2).reshape(2, boxes * half, rhs)]
    reshape x1 -> x2, local copies, waits for them, and re-layouts: 2.97 us -> 4.06 us  [the longest x1 2.97 us: on_device(): return field.transpose(1, 5, 2, 3, 0, 4).reshape(2, boxes * half, rhs)]
  transfers between devices with their start and end apart: 6 -> 0, of which waited for: 3 -> 0; matrix products, arithmetic and copies ran while one was open for 0% -> 0% of each run, Pallas kernels for 12% -> 0%
where the time goes in v1:
time: 50.7 us; the launch traced here: 50.3 us
  Pallas kernels  39 us (77%)
  local copies, waits for them, and re-layouts  8.98 us (18%)
  blocking collectives  2.26 us (4%)
    pallas_call x3, Pallas kernels, call(): pl.pallas_call(body, out_shape=out_shape, in_specs=[VM] * len(operands),...  39 us
    unnamed x14, local copies, waits for them, and re-layouts  4.06 us
    reshape x1, local copies, waits for them, and re-layouts, on_device(): return field.transpose(1, 5, 2, 3, 0, 4).reshape(2, boxes * half, rhs)  2.97 us
    all_gather x1, blocking collectives, on_device(): leaves = lax.all_gather(halves, 'src', axis=0, tiled=True)  2.26 us
    reshape x1, local copies, waits for them, and re-layouts, on_device(): field = field.reshape(CHUNKS, 2, half, src_count, group // src_count, boxes)  1.08 us

profile of v1, /device:TPU:0, one launch (start us, length us, event | category | flops | bytes accessed | tf_op | source)
XLA Modules:
  0.0 50.3 jit_solution(15466688202122104399)
XLA Ops:
  0.0 0.8 %reshape.12 = s32[128,32]{1,0:T(8,128)S(1)} reshape(s32[4096]{0:T(1024)} %param.8) | data formatting | bytes 32768 | tf_op jit(solution)/shard_map/reshape | solution.py:276
  0.8 0.0 copy-start.1
  0.8 0.0 copy-start.4
  0.8 0.1 copy.11
  0.9 0.0 copy-start.5
  0.9 1.0 %copy-done.5 = bf16[4096,32]{0,1:T(8,128)(2,1)S(1)} copy-done((bf16[4096,32]{0,1:T(8,128)(2,1)S(1)}, bf16[4096,32]{0,1:T(8,128)(2,1)}, u32[]{:S(2)}) %copy-start.5) | copy-done | bytes 262168
  1.9 4.0 %shard_map.73 = bf16[32,32,128]{2,1,0:T(8,128)(2,1)S(1)} custom-call(bf16[32,4096]{1,0:T(8,128)(2,1)S(1)} %bitcast.16, s32[16,256]{1,0:T(8,128)S(1)} %reshape.13.idx_ref), custom_call_target="tpu_custom_call" | custom-call | tf_op jit(solution)/shard_map/pallas_call | solution.py:253
  5.9 2.3 %all_gather.3.refs_0_.refs_2_ = bf16[64,32,128]{2,1,0:T(8,128)(2,1)S(1)} all-gather(bf16[32,32,128]{2,1,0:T(8,128)(2,1)S(1)} %shard_map.73), channel_id=1, replica_groups=mesh['grp'=2,'tgt'=8,'src'=2] {'src'}, dimensions={0}, use_global_device_ids=true | all-gather | bytes 786432 | tf_op jit(solution)/shard_map/all_gather | solution.py:281
  8.2 0.0 copy-start
  8.2 1.1 %copy-done = f32[2,10,2,32,64]{4,3,2,1,0:T(8,128)S(1)} copy-done((f32[2,10,2,32,64]{4,3,2,1,0:T(8,128)S(1)}, f32[2,10,2,32,64]{4,3,2,1,0:T(8,128)}, u32[]{:S(2)}) %copy-start) | copy-done | bytes 327704
  9.2 0.0 copy-start.2
  9.2 1.2 %copy-done.2 = bf16[2,128,32,64]{1,3,2,0:T(8,128)(2,1)S(1)} copy-done((bf16[2,128,32,64]{1,3,2,0:T(8,128)(2,1)S(1)}, bf16[2,128,32,64]{1,3,2,0:T(8,128)(2,1)}, u32[]{:S(2)}) %copy-start.2) | copy-done | bytes 1048600
  10.5 0.0 copy-start.6
  10.5 0.7 %copy-done.6 = s32[128,32]{0,1:T(8,128)S(1)} copy-done((s32[128,32]{0,1:T(8,128)S(1)}, s32[128,32]{0,1:T(8,128)}, u32[]{:S(2)}) %copy-start.6) | copy-done | bytes 16408
  11.2 0.0 copy-start.3
  11.2 5.1 %shard_map.74.refs_1_ = f32[64,2048]{1,0:T(8,128)S(1)} custom-call(bf16[64,32,128]{2,1,0:T(8,128)(2,1)S(1)} %all_gather.3.refs_0_.refs_2_, s32[32,128]{1,0:T(8,128)S(1)} %bitcast.17, bf16[2,32,64,128]{3,2,1,0:T(8,128)(2,1)S(1)} %bitcast.13, f32[2,10,2,32,64]{4,3,2,1,0:T(8,128)S(1)} %copy-done), custom_call_target="tpu_custom_call" | custom-call | tf_op jit(solution)/shard_map/pallas_call | solution.py:253
  16.3 0.0 copy-done.1
  16.3 0.0 copy-done.4
  16.3 0.0 copy-done.3
  16.3 29.9 %shard_map.75 = bf16[4,2,32,8,128]{4,3,2,1,0:T(8,128)(2,1)S(1)} custom-call(f32[2,10,2,32,64]{4,3,2,1,0:T(8,128)S(1)} %copy-done.1, f32[64,2048]{1,0:T(8,128)S(1)} %shard_map.74.refs_1_, bf16[64,32,128]{2,1,0:T(8,128)(2,1)S(1)} %all_gather.3.refs_0_.refs_2_, bf16[2,32,64,128]{3,2,1,0:T(8,128)(2,1)S(1)} %bitcast.14, bf16[2,32,32,128]{3,2,1,0:T(8,128)(2,1)S(1)} %bitcast.15), custom_call_target="tpu_custom_call" | custom-call | tf_op jit(solution)/shard_map/pallas_call | solution.py:253
  46.3 1.1 %copy.12 = bf16[4,2,32,2,4,128]{2,5,4,0,3,1:T(8,128)(2,1)S(1)} copy(bf16[4,2,32,2,4,128]{5,4,3,2,1,0:T(4,128)(2,1)S(1)} %bitcast.12) | data formatting | bytes 1048576 | tf_op jit(solution)/shard_map/reshape | solution.py:314
  47.4 3.0 %reshape.15 = bf16[2,4096,32]{1,2,0:T(8,128)(2,1)} reshape(bf16[2,128,32,2,4,4]{2,1,5,4,3,0:T(8,128)(2,1)S(1)} %bitcast.18) | data formatting | bytes 1048576 | tf_op jit(solution)/shard_map/reshape | solution.py:315
  (1 shorter events, 0.0 us)
Async XLA Ops:
  0.8 15.5 %copy-start.1 = (f32[2,10,2,32,64]{4,3,2,1,0:T(8,128)S(1)}, f32[2,10,2,32,64]{4,3,2,1,0:T(8,128)}, u32[]{:S(2)}) copy-start(f32[2,10,2,32,64]{4,3,2,1,0:T(8,128)} %refs_0_.1) | copy-start | bytes 983044
  0.8 15.5 %copy-start.4 = (bf16[2,128,32,32]{1,3,2,0:T(8,128)(2,1)S(1)}, bf16[2,128,32,32]{1,3,2,0:T(8,128)(2,1)}, u32[]{:S(2)}) copy-start(bf16[2,128,32,32]{1,3,2,0:T(8,128)(2,1)} %param.12) | copy-start | bytes 1572868
  0.9 1.0 %copy-start.5 = (bf16[4096,32]{0,1:T(8,128)(2,1)S(1)}, bf16[4096,32]{0,1:T(8,128)(2,1)}, u32[]{:S(2)}) copy-start(bf16[4096,32]{0,1:T(8,128)(2,1)} %param.7) | copy-start | bytes 786436
  8.2 1.1 %copy-start = (f32[2,10,2,32,64]{4,3,2,1,0:T(8,128)S(1)}, f32[2,10,2,32,64]{4,3,2,1,0:T(8,128)}, u32[]{:S(2)}) copy-start(f32[2,10,2,32,64]{4,3,2,1,0:T(8,128)} %refs_0_.1) | copy-start | bytes 983044
  9.2 1.2 %copy-start.2 = (bf16[2,128,32,64]{1,3,2,0:T(8,128)(2,1)S(1)}, bf16[2,128,32,64]{1,3,2,0:T(8,128)(2,1)}, u32[]{:S(2)}) copy-start(bf16[2,128,32,64]{1,3,2,0:T(8,128)(2,1)} %param.10) | copy-start | bytes 3145732
  10.5 0.7 %copy-start.6 = (s32[128,32]{0,1:T(8,128)S(1)}, s32[128,32]{0,1:T(8,128)}, u32[]{:S(2)}) copy-start(s32[128,32]{0,1:T(8,128)} %param.9) | copy-start | bytes 49156
  11.2 5.2 %copy-start.3 = (bf16[2,128,32,64]{1,3,2,0:T(8,128)(2,1)S(1)}, bf16[2,128,32,64]{1,3,2,0:T(8,128)(2,1)}, u32[]{:S(2)}) copy-start(bf16[2,128,32,64]{1,3,2,0:T(8,128)(2,1)} %param.11) | copy-start | bytes 3145732

commit v2 on v1

v2 whole, which is shorter than its diff:
```python
import jax
import jax.numpy as jnp
from jax import lax
from jax.experimental import pallas as pl
from jax.experimental.pallas import tpu as pltpu
from jax.sharding import PartitionSpec as P

F32 = jnp.float32
BF16 = jnp.bfloat16
CHUNKS = 4
LOW = 256
def split(value):
    high = value.astype(BF16)
    return high, (value - high.astype(F32)).astype(BF16)


def level_block(lm_ref, level, upper):
    real = lm_ref[0, level, upper]
    imag = lm_ref[1, level, upper]
    top = jnp.concatenate([real, -imag], axis=1)
    bottom = jnp.concatenate([imag, real], axis=1)
    return jnp.concatenate([top, bottom], axis=0)


def join(lower, higher):
    half = lower.shape[0] // 2
    return jnp.concatenate([lower[:half], higher[:half], lower[half:], higher[half:]], axis=0)


def dot(a, b):
    return jnp.dot(a, b, preferred_element_type=F32)


def dot3(a, b):
    a_high, a_low = split(a)
    b_high, b_low = split(b)
    return dot(a_high, b_high) + dot(a_high, b_low) + dot(a_low, b_high)


def partner_of(axis, bit_index):
    me = lax.axis_index(axis)
    mask = 2**bit_index
    return {axis: me + mask - 2 * mask * ((me // mask) % 2)}


def plan(bit_count):
    steps = [(bit, n) for bit in range(bit_count) for n in range(CHUNKS)]
    return sorted(steps, key=lambda at: at[1] + 1.5 * at[0] + (at[0] == bit_count - 1))


def column_index(order, rhs_rows):
    rows, lanes = order.shape
    turned = order.astype(F32).T.astype(BF16)
    per = lanes // rhs_rows
    at_row = lax.broadcasted_iota(jnp.int32, (rows, rows * per), 0)
    at_lane = lax.broadcasted_iota(jnp.int32, (rows, rows * per), 1)
    total = jnp.zeros((rhs_rows, rows * per), F32)
    for k in range(per):
        place = jnp.where(at_lane == at_row * per + k, 1.0, 0.0).astype(BF16)
        total = total + dot(turned[k * rhs_rows:(k + 1) * rhs_rows], place)
    return total.astype(jnp.int32)


def kernel(local_levels, bit_count, sources_hbm, order_hbm, skel_hbm, interp_hbm, tiles_hbm, basis_hbm, maps_hbm,
           out_ref,
           src_ref, order_ref, skel_ref, interp_ref, tiles_ref, basis_ref, lm_ref,
           table, low_ref, high_ref, halves, others, own_wide, weights, coeff_rows, maps_both, maps_low,
           vals, sent, came, mine, theirs, wide, near, basis, coeff, turned,
           in_sem, send_sem, recv_sem, half_send, half_recv):
    half, rhs, boxes = halves.shape
    points = wide.shape[0]
    rank = skel_ref.shape[0]
    size = vals.shape[2]
    per = size // boxes
    group = rhs // CHUNKS
    sources = group // per
    width = rhs // sources
    my_src = lax.axis_index("src")

    pairs = (
        (sources_hbm, src_ref), (order_hbm, order_ref), (maps_hbm, lm_ref), (skel_hbm, skel_ref),
        (interp_hbm, interp_ref), (tiles_hbm, tiles_ref), (basis_hbm, basis_ref),
    )
    loads = [pltpu.make_async_copy(a, b, in_sem.at[k]) for k, (a, b) in enumerate(pairs)]
    for load in loads:
        load.start()

    barrier = pltpu.get_barrier_semaphore()
    peers = [partner_of("tgt", bit) for bit in range(bit_count)] + [partner_of("src", 0)]
    for peer in peers:
        pl.semaphore_signal(barrier, inc=1, device_id=peer, device_id_type=pl.DeviceIdType.MESH)

    loads[1].wait()
    order = order_ref[...]
    low_ref[...] = column_index(order % LOW, half)
    high_ref[...] = column_index(order // LOW, half)
    loads[0].wait()
    high_count = src_ref.shape[1] // LOW
    for high in range(high_count):
        table[pl.ds(high * rhs, rhs), :] = src_ref[:, pl.ds(high * LOW, LOW)]
    together = LOW // boxes

    def gather_step(g, carry):
        low = jnp.concatenate([low_ref[pl.ds(g * together + k, 1), :] for k in range(together)], axis=1)
        high_at = jnp.concatenate([high_ref[pl.ds(g * together + k, 1), :] for k in range(together)], axis=1)
        high_of = jnp.broadcast_to(high_at, (rhs, LOW))
        rows = lax.broadcasted_iota(jnp.int32, (LOW, LOW), 0)
        onehot = jnp.where(rows == low, 1.0, 0.0).astype(BF16)
        found = dot(table[...], onehot)
        total = jnp.zeros((rhs, LOW), F32)
        for high in range(high_count):
            total = jnp.where(high_of == high, found[high * rhs:(high + 1) * rhs], total)
        for k in range(together):
            halves[g * together + k] = total[:, k * boxes:(k + 1) * boxes].astype(BF16)
        return carry

    pieces = 2
    piece_rows = half // pieces

    def half_copy(k):
        return pltpu.make_async_remote_copy(
            src_ref=halves.at[pl.ds(k * piece_rows, piece_rows)],
            dst_ref=others.at[pl.ds(k * piece_rows, piece_rows)],
            send_sem=half_send.at[k],
            recv_sem=half_recv.at[k],
            device_id=peers[bit_count],
            device_id_type=pl.DeviceIdType.MESH,
        )

    steps = piece_rows // together
    for k in range(pieces):
        lax.fori_loop(k * steps, (k + 1) * steps, gather_step, 0)
        if k == 0:
            pl.semaphore_wait(barrier, len(peers))
        half_copy(k).start()

    loads[2].wait()
    for level in range(local_levels):
        full = jnp.concatenate([level_block(lm_ref, level, 0), level_block(lm_ref, level, 1)], axis=0)
        a_high, a_low = split(full)
        maps_both[level] = jnp.concatenate([a_high, a_high], axis=1)
        maps_low[level] = a_low

    def spread(ref, at):
        rows = pl.ds(pl.multiple_of(at * half, half), half)
        own_wide[rows] = ref[:, pl.ds(pl.multiple_of(my_src * width, width), width), :].astype(F32)
        for n in range(CHUNKS):
            for s in range(sources):
                start = s * width + n * per
                wide[rows, n * group + s * per:n * group + (s + 1) * per, :] = (
                    ref[...].astype(F32)[:, start:start + per, :]
                )

    spread(halves, my_src)
    for k in range(pieces):
        half_copy(k).wait_recv()
    spread(others, 1 - my_src)

    loads[3].wait()
    loads[4].wait()
    block = weights.shape[0] // 2
    leaf_rows = lax.broadcasted_iota(jnp.int32, (points, boxes), 0)

    def rank_step(g, carry):
        for k in range(block):
            r = g * block + k
            pick = jnp.where(leaf_rows == skel_ref[pl.ds(r, 1), :], 1.0, 0.0)
            weights[2 * k] = interp_ref[0, r].astype(F32) + pick
            weights[2 * k + 1] = interp_ref[1, r].astype(F32)
        acc = jnp.zeros((2 * block, width, boxes), F32)
        for j in range(points):
            acc = acc + weights[:, j:j + 1, :] * own_wide[j][None]
        for k in range(block):
            for c in range(2):
                at = pl.multiple_of((c * rank + g * block + k) * width, width)
                coeff_rows[pl.ds(at, width), :] = acc[2 * k + c]
        return carry

    lax.fori_loop(0, rank // block, rank_step, 0)

    def copy_of(bit, n):
        inside = bit < bit_count
        return pltpu.make_async_remote_copy(
            src_ref=sent.at[bit, n] if inside else mine.at[n],
            dst_ref=came.at[bit, n] if inside else theirs.at[n],
            send_sem=send_sem.at[bit, n],
            recv_sem=recv_sem.at[bit, n],
            device_id=peers[bit],
            device_id_type=pl.DeviceIdType.MESH,
        )

    lane = lax.broadcasted_iota(jnp.int32, (2 * rank, boxes), 1)
    for first in range(0, CHUNKS, 2):
        chunks = range(first, min(first + 2, CHUNKS))
        for n in chunks:
            for h in range(per):
                vals[n, :, h * boxes:(h + 1) * boxes] = coeff_rows[pl.ds(n * per + h, 2 * rank, stride=width), :]
        for level in range(local_levels):
            distance = 2**level
            bit = (lane // distance) % 2 == 1
            for n in chunks:
                for q in range(0, size, LOW):
                    lows, highs = [], []
                    for at in range(q, q + LOW, boxes):
                        v = vals[n, :, at:at + boxes]
                        lows.append(jnp.where(bit, pltpu.roll(v, distance, 1), v))
                        highs.append(jnp.where(bit, v, pltpu.roll(v, boxes - distance, 1)))
                    stacked = join(jnp.concatenate(lows, axis=1), jnp.concatenate(highs, axis=1))
                    s_high, s_low = split(stacked)
                    both = jnp.concatenate([s_high, s_low], axis=0)
                    mixed = dot(maps_both[level], both) + dot(maps_low[level], s_high)
                    for k, at in enumerate(range(q, q + LOW, boxes)):
                        piece = mixed[:, k * boxes:(k + 1) * boxes]
                        vals[n, :, at:at + boxes] = jnp.where(bit, piece[2 * rank:], piece[:2 * rank])
        for n in chunks:
            sent[0, n] = vals[n].astype(BF16)
            copy_of(0, n).start()

    near_block = 2
    loads[5].wait()

    def near_step(g, carry):
        for k in range(near_block):
            for c in range(2):
                weights[2 * k + c] = tiles_ref[c, g * near_block + k].astype(F32)
        acc = jnp.zeros((2 * near_block, rhs, boxes), F32)
        for j in range(points):
            acc = acc + weights[:2 * near_block, j:j + 1, :] * wide[j][None]
        for k in range(near_block):
            for c in range(2):
                for n in range(CHUNKS):
                    at = pl.multiple_of((g * near_block + k) * group, group)
                    near[n, c, pl.ds(at, group), :] = acc[2 * k + c, n * group:(n + 1) * group]
        return carry

    near_total = half // near_block
    done = 0

    def near_part(count):
        nonlocal done
        end = min(near_total, done + count)
        if end > done:
            lax.fori_loop(done, end, near_step, 0)
        done = end

    src_first = jnp.broadcast_to(my_src, (2 * rank, size)) == 0
    box_of = lax.broadcasted_iota(jnp.int32, (half, boxes), 1)
    fold = boxes // half
    gathered = jnp.where(
        lax.broadcasted_iota(jnp.int32, (half, boxes), 0) == box_of // fold, 1.0, 0.0
    ).astype(BF16)

    def far_part(n):
        copy_of(bit_count, n).wait_recv()
        own = mine[n].astype(F32)
        other = theirs[n].astype(F32)
        for s, piece in enumerate((jnp.where(src_first, own, other), jnp.where(src_first, other, own))):
            for h in range(per):
                coeff[n, pl.ds(s * per + h, 2 * rank, stride=group), :] = piece[:, h * boxes:(h + 1) * boxes]
        many = 8

        def far_step(g, carry):
            rows = pl.ds(pl.multiple_of(g * many, many), many)
            flat = pl.ds(pl.multiple_of(g * many * group, many * group), many * group)
            real_acc = near[n, 0, flat, :].reshape(many, group, boxes)
            imag_acc = near[n, 1, flat, :].reshape(many, group, boxes)
            for r in range(rank):
                real = coeff[n, r * group:(r + 1) * group, :][None]
                imag = coeff[n, (rank + r) * group:(rank + r + 1) * group, :][None]
                w_real = basis[0, rows, r:r + 1, :]
                w_imag = basis[1, rows, r:r + 1, :]
                real_acc = real_acc + w_real * real - w_imag * imag
                imag_acc = imag_acc + w_real * imag + w_imag * real
            near[n, 0, flat, :] = real_acc.reshape(many * group, boxes)
            near[n, 1, flat, :] = imag_acc.reshape(many * group, boxes)
            return carry

        lax.fori_loop(0, half // many, far_step, 0)
        for c in range(2):
            for s in range(sources):
                for h in range(per):
                    plane = near[n, c, pl.ds(s * per + h, half, stride=group), :]
                    masked = [jnp.where(box_of % fold == k, plane, 0.0).astype(BF16) for k in range(fold)]
                    moved = lax.dot_general(
                        gathered, jnp.concatenate(masked, axis=0), (((1,), (1,)), ((), ())),
                        preferred_element_type=F32,
                    )
                    at = (s * width + n * per + h) * half
                    turned[c, at:at + half, :] = moved

    slots = [5, 3, 3, 2, 2]
    for at, (bit, n) in enumerate(plan(bit_count)):
        last = bit == bit_count - 1
        if last and n == 0:
            near_part(near_total)
            loads[6].wait()
            basis[...] = basis_ref[...].astype(F32)
        elif at < len(slots):
            near_part(slots[at])
        copy_of(bit, n).wait_recv()
        upper = (lax.axis_index("tgt") // 2**bit) % 2
        own = vals[n]
        other = came[bit, n].astype(F32)
        is_upper = jnp.broadcast_to(upper, own.shape) == 1
        stacked = join(jnp.where(is_upper, other, own), jnp.where(is_upper, own, other))
        mixed = dot3(level_block(lm_ref, local_levels + bit, upper), stacked)
        if last:
            mine[n] = mixed.astype(BF16)
        else:
            vals[n] = mixed
            sent[bit + 1, n] = mixed.astype(BF16)
        copy_of(bit + 1, n).start()
        if last:
            far_part(n)
    lanes = fold * half
    for c in range(2):
        for t in range(half):
            out_ref[c, :, t * lanes:(t + 1) * lanes] = turned[c, pl.ds(t, rhs, stride=half), :].astype(BF16)
    for k in range(pieces):
        half_copy(k).wait_send()
    for bit in range(bit_count + 1):
        for n in range(CHUNKS):
            copy_of(bit, n).wait_send()


def on_device(sources, leaf_order, skeleton, interp_rows, near_tiles, target_basis, level_maps):
    tgt_count = lax.axis_size("tgt")
    src_count = lax.axis_size("src")
    point_count, rhs = sources.shape
    boxes, rank = skeleton.shape
    leaf = interp_rows.shape[3]
    half = leaf // src_count
    width = rhs // src_count
    size = width * boxes // CHUNKS
    group = rhs // CHUNKS
    local_levels = boxes.bit_length() - 1
    bits = tgt_count.bit_length() - 1
    operands = (
        sources.T, leaf_order.reshape(point_count // boxes, boxes), skeleton.T,
        interp_rows.transpose(0, 2, 3, 1), near_tiles.transpose(0, 2, 3, 1),
        target_basis.transpose(0, 2, 3, 1), level_maps,
    )
    vmem = pltpu.VMEM
    dma = pltpu.SemaphoreType.DMA
    field = pl.pallas_call(
        lambda *refs: kernel(local_levels, bits, *refs),
        out_shape=jax.ShapeDtypeStruct((2, rhs, point_count), BF16),
        in_specs=[pl.BlockSpec(memory_space=pl.ANY)] * len(operands),
        out_specs=pl.BlockSpec(memory_space=pltpu.VMEM),
        scratch_shapes=[vmem(operand.shape, operand.dtype) for operand in operands] + [
            vmem((point_count // LOW * rhs, LOW), BF16),
            vmem((half, boxes), jnp.int32),
            vmem((half, boxes), jnp.int32),
            vmem((half, rhs, boxes), BF16),
            vmem((half, rhs, boxes), BF16),
            vmem((leaf, width, boxes), F32),
            vmem((8, leaf, boxes), F32),
            vmem((2 * rank * width, boxes), F32),
            vmem((local_levels, 4 * rank, 8 * rank), BF16),
            vmem((local_levels, 4 * rank, 4 * rank), BF16),
            vmem((CHUNKS, 2 * rank, size), F32),
            vmem((bits, CHUNKS, 2 * rank, size), BF16),
            vmem((bits, CHUNKS, 2 * rank, size), BF16),
            vmem((CHUNKS, 2 * rank, size), BF16),
            vmem((CHUNKS, 2 * rank, size), BF16),
            vmem((leaf, rhs, boxes), F32),
            vmem((CHUNKS, 2, half * group, boxes), F32),
            vmem((2, half, rank, boxes), F32),
            vmem((CHUNKS, 2 * rank * group, boxes), F32),
            vmem((2, rhs * half, boxes), F32),
            dma((len(operands),)),
            dma((bits + 1, CHUNKS)),
            dma((bits + 1, CHUNKS)),
            dma((2,)),
            dma((2,)),
        ],
        compiler_params=pltpu.CompilerParams(
            vmem_limit_bytes=60 * 2**20, collective_id=0, has_side_effects=True
        ),
    )(*operands)
    return field.transpose(0, 2, 1)


def solution(mesh):
    return jax.shard_map(
        on_device,
        mesh=mesh,
        in_specs=(
            P(("grp", "tgt", "src"), None),
            P(("grp", "tgt", "src")),
            P(("grp", "tgt"), None),
            P(None, ("grp", "tgt"), None, None),
            P(None, ("grp", "tgt"), "src", None),
            P(None, ("grp", "tgt"), "src", None),
            P(None, "grp", None, None, None),
        ),
        out_specs=P(None, ("grp", "tgt", "src"), None),
        check_vma=False,
    )
```

time: 50.7 us -> 44.9 us (0.89)
  local copies, waits for them, and re-layouts: 8.98 us -> 1.87 us
  Pallas kernels: 39 us -> 42.9 us
  blocking collectives: 2.26 us -> 0 us
    reshape x4 -> x0, local copies, waits for them, and re-layouts: 4.86 us -> none  [the longest x1 2.97 us: on_device(): return field.transpose(1, 5, 2, 3, 0, 4).reshape(2, boxes * half, rhs)]
    pallas_call x3 -> x1, Pallas kernels: 39 us -> 42.9 us  [on_device(): pl.pallas_call(lambda *refs: kernel(local_levels, bits, *refs), out_shape...]
    all_gather x1 -> x0, blocking collectives: 2.26 us -> none  [on_device(): leaves = lax.all_gather(halves, 'src', axis=0, tiled=True)]
    unnamed x14 -> x1, local copies, waits for them, and re-layouts: 4.06 us -> 1.87 us
where the time goes in v2:
time: 44.9 us; the launch traced here: 44.8 us
  Pallas kernels  42.9 us (96%)
  local copies, waits for them, and re-layouts  1.87 us (4%)
    pallas_call x1, Pallas kernels, on_device(): pl.pallas_call(lambda *refs: kernel(local_levels, bits, *refs), out_shape...  42.9 us
    unnamed x1, local copies, waits for them, and re-layouts  1.87 us

profile of v2, /device:TPU:0, one launch (start us, length us, event | category | flops | bytes accessed | tf_op | source)
XLA Modules:
  0.0 44.8 jit_solution(6829085566689550568)
XLA Ops:
  0.0 42.9 %shard_map.73 = bf16[2,32,4096]{2,1,0:T(8,128)(2,1)} custom-call(bf16[32,4096]{1,0:T(8,128)(2,1)} %bitcast.11, s32[32,128]{1,0:T(8,128)} %bitcast.12, s32[32,128]{1,0:T(8,128)} %bitcast.13, bf16[2,32,64,128]{3,2,1,0:T(8,128)(2,1)} %bitcast.8, bf16[2,32,64,128]{3,2,1,0:T(8,128)(2,1)} %bitcast.9, bf16[2,32,32,128]{3,2,1,0:T(8,128)(2,1)} %bitcast.10, ...), custom_call_target="tpu_custom_call" | custom-call | tf_op jit(solution)/shard_map/pallas_call | solution.py:345
  42.9 1.9 %copy.9 = bf16[2,4096,32]{1,2,0:T(8,128)(2,1)} copy(bf16[2,4096,32]{1,2,0:T(8,128)(2,1)} %bitcast.7) | data formatting | bytes 1048576

commit v3 on v2

--- a/solution.py
+++ b/solution.py
@@ -29,12 +29,6 @@
 
 def dot(a, b):
     return jnp.dot(a, b, preferred_element_type=F32)
-
-
-def dot3(a, b):
-    a_high, a_low = split(a)
-    b_high, b_low = split(b)
-    return dot(a_high, b_high) + dot(a_high, b_low) + dot(a_low, b_high)
 
 
 def partner_of(axis, bit_index):
@@ -64,7 +58,7 @@
 def kernel(local_levels, bit_count, sources_hbm, order_hbm, skel_hbm, interp_hbm, tiles_hbm, basis_hbm, maps_hbm,
            out_ref,
            src_ref, order_ref, skel_ref, interp_ref, tiles_ref, basis_ref, lm_ref,
-           table, low_ref, high_ref, halves, others, own_wide, weights, coeff_rows, maps_both, maps_low,
+           table, low_ref, high_ref, halves, others, own_wide, weights, coeff_rows, maps_both, maps_low, cross_high, cross_low,
            vals, sent, came, mine, theirs, wide, near, basis, coeff, turned,
            in_sem, send_sem, recv_sem, half_send, half_recv):
     half, rhs, boxes = halves.shape
@@ -140,6 +134,10 @@
         a_high, a_low = split(full)
         maps_both[level] = jnp.concatenate([a_high, a_high], axis=1)
         maps_low[level] = a_low
+
+    for bit in range(bit_count):
+        upper = (lax.axis_index("tgt") // 2**bit) % 2
+        cross_high[bit], cross_low[bit] = split(level_block(lm_ref, local_levels + bit, upper))
 
     def spread(ref, at):
         rows = pl.ds(pl.multiple_of(at * half, half), half)
@@ -218,6 +216,7 @@
 
     near_block = 2
     loads[5].wait()
+    near[...] = jnp.zeros(near.shape, F32)
 
     def near_step(g, carry):
         for k in range(near_block):
@@ -230,7 +229,8 @@
             for c in range(2):
                 for n in range(CHUNKS):
                     at = pl.multiple_of((g * near_block + k) * group, group)
-                    near[n, c, pl.ds(at, group), :] = acc[2 * k + c, n * group:(n + 1) * group]
+                    rows = pl.ds(at, group)
+                    near[n, c, rows, :] = near[n, c, rows, :] + acc[2 * k + c, n * group:(n + 1) * group]
         return carry
 
     near_total = half // near_block
@@ -276,6 +276,8 @@
             return carry
 
         lax.fori_loop(0, half // many, far_step, 0)
+
+    def turn_part(n):
         for c in range(2):
             for s in range(sources):
                 for h in range(per):
@@ -288,11 +290,10 @@
                     at = (s * width + n * per + h) * half
                     turned[c, at:at + half, :] = moved
 
-    slots = [5, 3, 3, 2, 2]
+    slots = [4, 2, 2, 1, 1]
     for at, (bit, n) in enumerate(plan(bit_count)):
         last = bit == bit_count - 1
         if last and n == 0:
-            near_part(near_total)
             loads[6].wait()
             basis[...] = basis_ref[...].astype(F32)
         elif at < len(slots):
@@ -303,7 +304,8 @@
         other = came[bit, n].astype(F32)
         is_upper = jnp.broadcast_to(upper, own.shape) == 1
         stacked = join(jnp.where(is_upper, other, own), jnp.where(is_upper, own, other))
-        mixed = dot3(level_block(lm_ref, local_levels + bit, upper), stacked)
+        s_high, s_low = split(stacked)
+        mixed = dot(cross_high[bit], s_high) + dot(cross_high[bit], s_low) + dot(cross_low[bit], s_high)
         if last:
             mine[n] = mixed.astype(BF16)
         else:
@@ -311,7 +313,13 @@
             sent[bit + 1, n] = mixed.astype(BF16)
         copy_of(bit + 1, n).start()
         if last:
+            if n < CHUNKS - 1:
+                near_part(near_total if n == CHUNKS - 2 else 2)
+            else:
+                for earlier in range(n):
+                    turn_part(earlier)
             far_part(n)
+    turn_part(CHUNKS - 1)
     lanes = fold * half
     for c in range(2):
         for t in range(half):
@@ -358,6 +366,8 @@
             vmem((2 * rank * width, boxes), F32),
             vmem((local_levels, 4 * rank, 8 * rank), BF16),
             vmem((local_levels, 4 * rank, 4 * rank), BF16),
+            vmem((bits, 2 * rank, 4 * rank), BF16),
+            vmem((bits, 2 * rank, 4 * rank), BF16),
             vmem((CHUNKS, 2 * rank, size), F32),
             vmem((bits, CHUNKS, 2 * rank, size), BF16),
             vmem((bits, CHUNKS, 2 * rank, size), BF16),

time: 44.9 us -> 43.5 us (0.969)
  Pallas kernels: 42.9 us -> 41.5 us
    pallas_call x1, Pallas kernels: 42.9 us -> 41.5 us  [on_device(): pl.pallas_call(lambda *refs: kernel(local_levels, bits, *refs), out_shape...]
where the time goes in v3:
time: 43.5 us; the launch traced here: 43.4 us
  Pallas kernels  41.5 us (95%)
  local copies, waits for them, and re-layouts  1.87 us (4%)
    pallas_call x1, Pallas kernels, on_device(): pl.pallas_call(lambda *refs: kernel(local_levels, bits, *refs), out_shape...  41.5 us
    unnamed x1, local copies, waits for them, and re-layouts  1.87 us

profile of v3, /device:TPU:0, one launch (start us, length us, event | category | flops | bytes accessed | tf_op | source)
XLA Modules:
  0.0 43.4 jit_solution(16246492774579762618)
XLA Ops:
  0.0 41.5 %shard_map.73 = bf16[2,32,4096]{2,1,0:T(8,128)(2,1)} custom-call(bf16[32,4096]{1,0:T(8,128)(2,1)} %bitcast.11, s32[32,128]{1,0:T(8,128)} %bitcast.12, s32[32,128]{1,0:T(8,128)} %bitcast.13, bf16[2,32,64,128]{3,2,1,0:T(8,128)(2,1)} %bitcast.8, bf16[2,32,64,128]{3,2,1,0:T(8,128)(2,1)} %bitcast.9, bf16[2,32,32,128]{3,2,1,0:T(8,128)(2,1)} %bitcast.10, ...), custom_call_target="tpu_custom_call" | custom-call | tf_op jit(solution)/shard_map/pallas_call | solution.py:353
  41.5 1.9 %copy.9 = bf16[2,4096,32]{1,2,0:T(8,128)(2,1)} copy(bf16[2,4096,32]{1,2,0:T(8,128)(2,1)} %bitcast.7) | data formatting | bytes 1048576
